TPU v7x, 128 devices: a whole 4x4x4 slice. The times are simulated.
128 devices in a mesh: leaf: 8 (over z, x_hi), grid: 16 (over y, x_lo, core).
Axes of the slice: x: 4 (x_hi: 2, x_lo: 2; x = x_hi * 2 + x_lo), y: 4, z: 4, core: 2. Of those that a mesh axis runs over, the one named last changes fastest.
Arguments:
- root_inverse: float32 [4096, 4096], P('grid', 'leaf'), may hold values from -1 to 12, as said below
- middle_inverse: float32 [2048, 4096], P('grid', 'leaf'), may hold values from -1 to 12, as said below
- middle_panel: float32 [4096, 4096], P('grid', 'leaf'), may hold values from -0.1875 to 0.1875
- lower_root: float32 [4096, 8192], P('grid', 'leaf'), may hold values from -0.1875 to 0.1875
- lower_middle: float32 [2048, 8192], P(None, 'leaf'), may hold values from -0.25 to 0.25
- block_pattern: int32 [4, 32], replicated, may hold values 0 or 1
- lower_diagonal: float32 [8192], P('leaf'), may hold values from 1.5 to 6
Outputs:
- middle_cross: float32 [4096, 4096], P('grid', 'leaf')
- middle_variance: float32 [4096], P('leaf')
- lower_cross: float32 [4096, 8192], P('grid', 'leaf')
- lower_parent: float32 [2048, 8192], P('grid', 'leaf')
- lower_variance: float32 [8192], P('leaf')
Inputs may be any that keep to these rules, and one draw needn't show every extreme that they name: `root_inverse`: symmetric; its diagonal entries lie between 1.5 and 12. `middle_inverse`: each front's 2048 x 2048 block is symmetric; its diagonal entries lie between 1.5 and 12.
All inputs are finite; a program needn't handle non-finite values.
Results may differ from a plain program's by a relative error of at most 0.0001.
Values sent between devices are 32-bit elements; how exact they have to be, the bound alone decides.
A program may use at most 128 MiB of HBM per device.

v0:
```python
import functools

import jax
import jax.numpy as jnp
from jax import lax
from jax.experimental import pallas as pl
from jax.experimental.pallas import tpu as pltpu
from jax.sharding import PartitionSpec as P

MESH = pl.DeviceIdType.MESH
F32 = jnp.float32
BF16 = jnp.bfloat16
MIB = 2**20


def device(z, a, y, b, c):
    return (z * 2 + a, y * 4 + b * 2 + c)


def flip(v, k):
    if k == 0:
        return v
    if k == 1:
        return v + 1 - 2 * (v % 2)
    if k == 2:
        return (v + 2) % 4
    return 3 - v


def either(u, v):
    return (u // 2 + v // 2) % 2 * 2 + (u + v) % 2


def high_low(x):
    high = x.astype(BF16)
    low = (x - high.astype(F32)).astype(BF16)
    return high, low


def kernel(
    s_hbm, minv_hbm, p_hbm, l_hbm, m_hbm, pattern, diag_ref,
    f_hbm, root_hbm, par_hbm, sum_out,
    s_buf, p_col, l_buf, frow, ft, f_part, f_recv, r_part, r_recv, q_part, q_recv, t_part, t_recv, t_row,
    m_stage, m_own, tm, fm, sums, relay, f_out,
    s_split, l_hi, l_lo, m_hi, m_lo, p_hi, p_lo, a_tmp, t_tmp, ft_split,
    loc, mst, x_s, x_r, z_s, z_r, py_s, py_r, ps_s, ps_r, ly_s, ly_r, ls_s, ls_r,
    fx_s, fx_r, fr_s, fr_r, ft_s, ft_r, rx_s, rx_r, qx_s, qx_r, tx_s, tx_r, tr_s, tr_r, sum_s, sum_r,
):
    leaf = lax.axis_index("leaf")
    grid = lax.axis_index("grid")
    z, a = leaf // 2, leaf % 2
    y, b, c = grid // 4, (grid // 2) % 2, grid % 2
    front, idx = z // 2, leaf % 4
    same = a == b
    differ = jnp.logical_not(same)
    here_rows = pl.ds(pl.multiple_of(c * 256, 256), 256)

    def half_rows(h):
        return pl.ds(pl.multiple_of(c * 256 + h * 128, 128), 128)

    def at_idx(k):
        return (front * 4 + flip(idx, k), grid)

    def at_y(k):
        return (leaf, flip(y, k) * 4 + grid % 4)

    def at_z(k):
        return (flip(z, k) * 2 + a, grid)

    sibling = (leaf, grid + 1 - 2 * c)
    partner = (leaf, y * 4 + (1 - b) * 2 + c)
    def remote(src, dst, ss, rs, dev):
        return pltpu.make_async_remote_copy(
            src_ref=src, dst_ref=dst, send_sem=ss, recv_sem=rs, device_id=dev, device_id_type=MESH
        )

    bar = pltpu.get_barrier_semaphore()

    def greet(dev):
        pl.semaphore_signal(bar, inc=1, device_id=dev, device_id_type=MESH)

    @pl.loop(1, 16)
    def _(k):
        greet((leaf, (grid + k) % 16))

    greet(at_z(1))
    greet(at_z(3))
    for k in range(1, 4):
        x = (a * 2 + b + k) % 4
        greet(device(z, x // 2, y, x % 2, c))
    pl.semaphore_wait(bar, 20)

    def own_s(h):
        return pltpu.make_async_copy(s_hbm.at[pl.ds(h * 128, 128)], s_buf.at[0, h, b], loc.at[h])

    def step(h, kind, n, dev):
        return remote(s_hbm.at[pl.ds(h * 128, 128)], s_buf.at[0, h, b], x_s.at[kind, h], x_r.at[n, h], dev)

    def step_one(h):
        return step(h, 0, 0, device(z, a, y, a, c))

    def step_two(h):
        return step(h, 1, 1, device(z, 1 - a, y, a, c))

    def step_out(h):
        return remote(s_hbm.at[pl.ds(h * 128, 128)], relay.at[h], x_s.at[0, h], x_r.at[1, h],
                      device(z, 1 - a, y, 1 - b, c))

    def step_on(h):
        return remote(relay.at[h], s_buf.at[0, h, 1 - b], x_s.at[1, h], x_r.at[0, h], device(z, a, y, 1 - b, c))

    def step_start(h):
        @pl.when(same)
        def _():
            own_s(h).start()
            step_out(h).start()

        @pl.when(differ)
        def _():
            step_one(h).start()
            step_two(h).start()

    def step_relay(h):
        @pl.when(same)
        def _():
            step_out(h).wait_recv()
            step_on(h).start()

    step_start(0)

    own_l = pltpu.make_async_copy(l_hbm, l_buf.at[0, here_rows], loc.at[4])
    own_l.start()

    def y_own(src, buf, ss, rs, h, k):
        return remote(src, buf.at[k, half_rows(h)], ss.at[h, k], rs.at[h, k], at_y(k))

    def y_on(buf, ss, rs, h):
        came, way = (1, 3) if h == 0 else (3, 1)
        return remote(buf.at[came, half_rows(h)], buf.at[2, half_rows(h)], ss.at[h, 2], rs.at[h, 2], at_y(way))

    def p_own(h, k):
        return y_own(p_hbm.at[pl.ds(h * 128, 128)], p_col, py_s, py_r, h, k)

    def l_own(h, k):
        return y_own(l_buf.at[0, half_rows(h)], l_buf, ly_s, ly_r, h, k)

    for h, k in ((0, 1), (1, 3), (1, 1), (0, 3)):
        p_own(h, k).start()
    own_p = pltpu.make_async_copy(p_hbm, p_col.at[0, here_rows], loc.at[2])
    own_p.start()
    own_t = pltpu.make_async_copy(minv_hbm, t_row.at[0], loc.at[3])
    own_m = pltpu.make_async_copy(m_hbm.at[pl.ds(pl.multiple_of(grid * 128, 128), 128)], m_own, loc.at[5])
    own_t.start()
    own_m.start()

    def m_load(i):
        return pltpu.make_async_copy(m_hbm.at[pl.ds(i * 256, 256)], m_stage.at[i % 2], mst.at[i % 2])

    m_load(0).start()
    m_load(1).start()

    def p_side(k):
        return remote(p_hbm if k == 0 else p_col.at[k, here_rows], p_col.at[k, here_rows],
                      ps_s.at[k], ps_r.at[k], sibling)

    def l_side(k):
        return remote(l_buf.at[k, here_rows], l_buf.at[k, here_rows], ls_s.at[k], ls_r.at[k], sibling)

    p_side(0).start()

    own_l.wait()
    for i in range(2):
        keep = pattern[leaf // 2, grid * 2 + i].astype(F32)
        l_buf[0, half_rows(i)] = l_buf[0, half_rows(i)] * keep

    def split_m(i):
        m_load(i).wait()

        @pl.loop(0, 8)
        def _(n):
            rows = pl.ds(pl.multiple_of(n * 32, 32), 32)
            to = pl.ds(pl.multiple_of(i % 2 * 256 + n * 32, 32), 32)
            hi, lo = high_low(m_stage[i % 2, rows])
            m_hi[i // 2, to] = hi
            m_lo[i // 2, to] = lo
        if i + 2 < 8:
            m_load(i + 2).start()

    def split_rows(src, hi_ref, lo_ref, k):
        for n, m in enumerate((0, 2, 1, 3)):
            @pl.loop(0, 4)
            def _(i):
                rows = pl.ds(pl.multiple_of(m * 128 + i * 32, 32), 32)
                to = pl.ds(pl.multiple_of(n * 128 + i * 32, 32), 32)
                hi, lo = high_low(src[k, rows])
                hi_ref[k, to] = hi
                lo_ref[k, to] = lo

    def split_s(k, h):
        for bb in range(2):
            hi, lo = high_low(s_buf[k, h, bb])
            for part, base in ((hi, 0), (lo, 256)):
                at = slice(base + bb * 128, base + bb * 128 + 128)
                for n, m in enumerate((0, 2, 1, 3)):
                    s_split[k, h, at, n * 128:n * 128 + 128] = part[:, m * 128:m * 128 + 128]

    def accumulate(acc, lhs, rhs_hi, rhs_lo, first):
        m, n = acc.shape
        width = min(n, 512)

        @pl.loop(0, n // width)
        def _(j):
            cols = pl.ds(pl.multiple_of(j * width, width), width)
            hi = rhs_hi[:, cols]
            part = jnp.dot(lhs[0:m], hi, preferred_element_type=F32)
            part += jnp.dot(lhs[m:2 * m], hi, preferred_element_type=F32)
            part += jnp.dot(lhs[0:m], rhs_lo[:, cols], preferred_element_type=F32)
            if first:
                acc[:, cols] = part
            else:
                acc[:, cols] += part

    def z_own(h, bb, k):
        return remote(s_buf.at[0, h, bb], s_buf.at[k, h, bb], z_s.at[h, bb, k], z_r.at[h, bb, k], at_z(k))

    def z_on(h, bb):
        came, way = (1, 3) if bb == 0 else (3, 1)
        return remote(s_buf.at[came, h, bb], s_buf.at[2, h, bb], z_s.at[h, bb, 2], z_r.at[h, bb, 2], at_z(way))

    def s_here(h):
        @pl.when(same)
        def _():
            own_s(h).wait()
            step_one(h).wait_recv()

        @pl.when(differ)
        def _():
            step_one(h).wait_recv()
            step_two(h).wait_recv()
        for bb, k in ((0, 1), (1, 3), (1, 1), (0, 3)):
            z_own(h, bb, k).start()

    def s_on(h):
        z_own(h, 0, 1).wait_recv()
        z_on(h, 0).start()
        z_own(h, 1, 3).wait_recv()
        z_on(h, 1).start()

    def f_chunk(h, k, first=False):
        split_s(k, h)
        ky = either(y, flip(z, k))
        accumulate(f_part.at[h], s_split.at[k, h], p_hi.at[ky], p_lo.at[ky], first)

    def f_near(h):
        for k, bb in ((1, 1), (3, 0)):
            z_own(h, bb, k).wait_recv()
            f_chunk(h, k)

    other_rows = pl.ds(pl.multiple_of((1 - b) * 128, 128), 128)
    own_rows = pl.ds(pl.multiple_of(b * 128, 128), 128)

    def fx(h):
        return remote(f_part.at[h, other_rows], f_recv.at[h], fx_s.at[h], fx_r.at[h], partner)

    def f_last(h):
        z_on(h, 0).wait_recv()
        z_on(h, 1).wait_recv()
        f_chunk(h, 2)
        fx(h).start()

    def fr(k, h):
        src = frow.at[1, h] if k == 3 else frow.at[0, h]
        return remote(src, frow.at[k, h], fr_s.at[k, h], fr_r.at[k, h], at_idx(1 if k == 1 else 2))

    def f_final(h):
        fx(h).wait_recv()
        whole = f_part[h, own_rows] + f_recv[h]
        for cc in range(2):
            for bb in range(2):
                at = bb * 256 + cc * 128
                frow[0, h, cc, :, bb * 128:bb * 128 + 128] = whole[:, at:at + 128]
        fr(1, h).start()
        fr(2, h).start()
        f_out[h * 128:h * 128 + 128] = -whole

    def ft_far(k, h, cc):
        return remote(frow.at[k, h, cc], ft.at[y, c, h], ft_s.at[h, k, cc], ft_r.at[h, y, c],
                      (leaf, flip(idx, k) * 4 + b * 2 + cc))

    def ft_near(k, h):
        return pltpu.make_async_copy(frow.at[k, h, c], ft.at[y, c, h], loc.at[6 + h])

    def ft_send(k, h):
        for cc in range(2):
            mine = (flip(idx, k) == y) & (c == cc)

            @pl.when(mine)
            def _():
                ft_near(k, h).start()

            @pl.when(jnp.logical_not(mine))
            def _():
                ft_far(k, h, cc).start()

    def fr_step(k, h):
        fr(k, h).wait_recv()
        if k == 1:
            fr(3, h).start()
        ft_send(k, h)

    def root_chunk(h, ky, first=False):
        kz = either(z, flip(y, ky))
        accumulate(r_part.at[h], s_split.at[kz, h], l_hi.at[ky], l_lo.at[ky], first)

    def rx(h):
        return remote(r_part.at[h, other_rows], r_recv.at[h], rx_s.at[h], rx_r.at[h], partner)

    def l_ready(k):
        l_side(k).wait_recv()
        split_rows(l_buf, l_hi, l_lo, k)

    split_m(0)
    split_m(1)
    step_relay(0)
    step_start(1)
    split_m(2)
    p_own(0, 1).wait_recv()
    y_on(p_col, py_s, py_r, 0).start()
    p_own(1, 3).wait_recv()
    y_on(p_col, py_s, py_r, 1).start()
    s_here(0)
    split_m(3)
    step_relay(1)
    p_own(1, 1).wait_recv()
    p_side(1).start()
    p_own(0, 3).wait_recv()
    p_side(3).start()
    for h, k in ((0, 1), (1, 3), (1, 1), (0, 3)):
        l_own(h, k).start()
    l_side(0).start()
    split_m(4)
    s_on(0)
    s_here(1)
    split_m(5)
    own_p.wait()
    for k in (0, 1, 3):
        p_side(k).wait_recv()
        split_rows(p_col, p_hi, p_lo, k)
    y_on(p_col, py_s, py_r, 0).wait_recv()
    y_on(p_col, py_s, py_r, 1).wait_recv()
    p_side(2).start()
    split_m(6)
    p_side(2).wait_recv()
    split_rows(p_col, p_hi, p_lo, 2)
    f_chunk(0, 0, True)
    s_on(1)
    f_near(0)
    split_m(7)
    f_last(0)
    f_chunk(1, 0, True)
    l_ready(0)
    l_own(0, 1).wait_recv()
    y_on(l_buf, ly_s, ly_r, 0).start()
    l_own(1, 3).wait_recv()
    y_on(l_buf, ly_s, ly_r, 1).start()
    f_final(0)
    ft_send(0, 0)
    root_chunk(0, 0, True)
    for k, h in ((1, 1), (3, 0)):
        l_own(h, k).wait_recv()
        l_side(k).start()
    f_near(1)
    l_ready(1)
    root_chunk(0, 1)
    l_ready(3)
    f_last(1)
    fr_step(1, 0)
    fr_step(2, 0)
    root_chunk(0, 3)
    y_on(l_buf, ly_s, ly_r, 0).wait_recv()
    y_on(l_buf, ly_s, ly_r, 1).wait_recv()
    l_side(2).start()
    f_final(1)
    f_done = pltpu.make_async_copy(f_out, f_hbm, loc.at[8])
    f_done.start()
    ft_send(0, 1)
    l_ready(2)
    root_chunk(0, 2)
    rx(0).start()
    fr_step(3, 0)
    root_chunk(1, 0, True)
    fr_step(1, 1)
    fr_step(2, 1)
    for k in (1, 3):
        root_chunk(1, k)
    fr_step(3, 1)
    root_chunk(1, 2)
    rx(1).start()

    tx = remote(t_part.at[other_rows], t_recv, tx_s.at[0], tx_r.at[0], partner)

    def tr(k):
        return remote(t_row.at[1] if k == 3 else t_row.at[0], t_row.at[k], tr_s.at[k], tr_r.at[k],
                      at_idx(1 if k == 1 else 2))

    def t_chunk(h, k, first):
        far = flip(y, k)
        for cc in range(2):
            came = remote(frow.at[0, h, cc], ft.at[far, cc, h], ft_s.at[h, 0, cc], ft_r.at[h, far, cc], sibling)
            if k == 0:
                @pl.when(c == cc)
                def _():
                    ft_near(0, h).wait()

                @pl.when(c != cc)
                def _():
                    came.wait_recv()
            else:
                came.wait_recv()
            hi, lo = high_low(ft[far, cc, h].T)
            ft_split[h, k, 0:256, cc * 128:cc * 128 + 128] = hi
            ft_split[h, k, 256:512, cc * 128:cc * 128 + 128] = lo
        rows = slice(h * 256, h * 256 + 256)
        accumulate(t_part, ft_split.at[h, k], p_hi.at[k, rows], p_lo.at[k, rows], first)

    def q_chunk(h, k, first):
        rows = slice(h * 256, h * 256 + 256)
        accumulate(q_part, ft_split.at[h, k], l_hi.at[k, rows], l_lo.at[k, rows], first)

    for k in (0, 1, 3, 2):
        t_chunk(0, k, k == 0)

    for k in range(4):
        for h in range(2):
            for cc in range(2):
                hi, lo = high_low(frow[k, h, cc])
                for bb in range(2):
                    at = bb * 256 + cc * 128
                    part = slice(bb * 128, bb * 128 + 128)
                    a_tmp[h * 128:h * 128 + 128, at:at + 128] = hi[:, part]
                    a_tmp[256 + h * 128:256 + h * 128 + 128, at:at + 128] = lo[:, part]
        accumulate(fm, a_tmp, m_hi.at[flip(idx, k)], m_lo.at[flip(idx, k)], k == 0)
    for k in (0, 1, 3, 2):
        q_chunk(0, k, k == 0)
    for k in (0, 1, 3, 2):
        t_chunk(1, k, False)
    tx.start()
    for k in (0, 1, 3, 2):
        q_chunk(1, k, False)
    own_t.wait()
    tx.wait_recv()
    t_row[0] = t_row[0] + (t_part[own_rows] + t_recv[...])
    tr(1).start()
    tr(2).start()
    qx = remote(q_part.at[other_rows], q_recv, qx_s.at[0], qx_r.at[0], partner)
    qx.start()

    row_at = grid * 128 + lax.broadcasted_iota(jnp.int32, (128, 512), 0)
    col_at = idx * 512 + lax.broadcasted_iota(jnp.int32, (128, 512), 1)
    mid = jnp.sum(jnp.where(row_at == col_at, t_row[0], 0.0), axis=0, keepdims=True)
    for i in range(4):
        sums[0, 8 + i:9 + i] = mid[:, i * 128:i * 128 + 128]
        sums[0, 12 + i:13 + i] = jnp.zeros((1, 128), F32)

    for k in range(4):
        if k:
            tr(k).wait_recv()
        if k == 1:
            tr(3).start()
        hi, lo = high_low(t_row[k])
        t_tmp[0:128] = hi
        t_tmp[128:256] = lo
        accumulate(tm, t_tmp, m_hi.at[flip(idx, k)], m_lo.at[flip(idx, k)], k == 0)

    def root_done(h):
        return pltpu.make_async_copy(r_recv.at[h], root_hbm.at[pl.ds(h * 128, 128)], loc.at[9 + h])

    low = jnp.zeros((1, 1024), F32)
    for h in range(2):
        rx(h).wait_recv()
        rows = slice(h * 128, h * 128 + 128)
        root = r_part[h, own_rows] + r_recv[h] - fm[rows]
        r_recv[h] = -root
        root_done(h).start()
        low += jnp.sum(l_buf[0, half_rows(h)] * root, axis=0, keepdims=True)
    own_m.wait()
    qx.wait_recv()
    par = tm[...] - (q_part[own_rows] + q_recv[...])
    q_recv[...] = -par
    par_done = pltpu.make_async_copy(q_recv, par_hbm, loc.at[11])
    par_done.start()
    low += jnp.sum(m_own[...] * par, axis=0, keepdims=True)
    for i in range(8):
        sums[0, i:i + 1] = low[:, i * 128:i * 128 + 128]

    def sum_copy(k):
        return remote(sums.at[0], sums.at[k], sum_s.at[k], sum_r.at[k], (leaf, (grid + k) % 16))

    for k in range(1, 16):
        sum_copy(k).start()
    total = sums[0]
    for k in range(1, 16):
        sum_copy(k).wait_recv()
    for k in range(1, 16):
        total += sums[k]
    sum_out[0:8] = total[0:8] + diag_ref[...]
    sum_out[8:16] = total[8:16]
    f_done.wait()
    for h in range(2):
        root_done(h).wait()
    par_done.wait()

    @pl.when(same)
    def _():
        for h in range(2):
            step_out(h).wait_send()
            step_on(h).wait_send()

    @pl.when(differ)
    def _():
        for h in range(2):
            step_one(h).wait_send()
            step_two(h).wait_send()
    for h in range(2):
        for k in (1, 3):
            p_own(h, k).wait_send()
            l_own(h, k).wait_send()
            for bb in range(2):
                z_own(h, bb, k).wait_send()
        y_on(p_col, py_s, py_r, h).wait_send()
        y_on(l_buf, ly_s, ly_r, h).wait_send()
        for bb in range(2):
            z_on(h, bb).wait_send()
    for k in range(4):
        p_side(k).wait_send()
        l_side(k).wait_send()
    for h in range(2):
        fx(h).wait_send()
        rx(h).wait_send()
        for k in range(4):
            if k:
                fr(k, h).wait_send()
            for cc in range(2):
                @pl.when(jnp.logical_not((flip(idx, k) == y) & (c == cc)))
                def _():
                    ft_far(k, h, cc).wait_send()
    tx.wait_send()
    for k in range(1, 4):
        tr(k).wait_send()
    qx.wait_send()
    for k in range(1, 16):
        sum_copy(k).wait_send()


def finish(first, root, par, total_hbm, first_out, mid_out, root_out, par_out, low_out, f_buf, r_buf, q_buf, total, sem):
    pairs = ((root, r_buf, root_out), (first, f_buf, first_out), (par, q_buf, par_out))
    come = [pltpu.make_async_copy(src, buf, sem.at[0, i]) for i, (src, buf, _) in enumerate(pairs)]
    go = [pltpu.make_async_copy(buf, dst, sem.at[1, i]) for i, (_, buf, dst) in enumerate(pairs)]
    sums = pltpu.make_async_copy(total_hbm, total, sem.at[0, 3])
    for copy in come:
        copy.start()
    sums.start()
    for i in range(3):
        come[i].wait()
        go[i].start()
    sums.wait()
    for i in range(8):
        low_out[i * 128:i * 128 + 128] = total[i]
    for i in range(4):
        mid_out[i * 128:i * 128 + 128] = total[8 + i]
    for copy in go:
        copy.wait()


def local(root_inverse, middle_inverse, middle_panel, lower_root, lower_middle, block_pattern, lower_diagonal):
    dma = pltpu.SemaphoreType.DMA
    vmem = pl.BlockSpec(memory_space=pltpu.VMEM)
    hbm = pl.BlockSpec(memory_space=pl.ANY)
    scratch = [
        pltpu.VMEM(shape, F32)
        for shape in (
            (4, 2, 2, 128, 512), (4, 512, 512), (4, 512, 1024), (4, 2, 2, 128, 256), (4, 2, 2, 128, 256),
            (2, 256, 512), (2, 128, 512), (2, 256, 1024), (2, 128, 1024), (256, 1024), (128, 1024),
            (256, 512), (128, 512), (4, 128, 512),
            (2, 256, 1024), (128, 1024), (128, 1024), (256, 1024), (16, 16, 128), (2, 128, 512),
            (256, 512),
        )
    ] + [
        pltpu.VMEM(shape, BF16)
        for shape in (
            (4, 2, 512, 512), (4, 512, 1024), (4, 512, 1024), (4, 512, 1024), (4, 512, 1024),
            (4, 512, 512), (4, 512, 512), (512, 512), (256, 512), (2, 4, 512, 256),
        )
    ] + [
        dma(shape)
        for shape in (
            (12,), (2,), (2, 2), (2, 2), (2, 2, 4), (2, 2, 4), (2, 4), (2, 4), (4,), (4,), (2, 4), (2, 4), (4,), (4,),
            (2,), (2,), (4, 2), (4, 2), (2, 4, 2), (2, 4, 2), (2,), (2,), (1,), (1,), (1,), (1,), (4,), (4,),
            (16,), (16,),
        )
    ]
    blocks = tuple(jax.ShapeDtypeStruct(shape, F32) for shape in ((256, 512), (256, 1024), (128, 1024)))
    first, root, par, total = pl.pallas_call(
        kernel,
        out_shape=blocks + (jax.ShapeDtypeStruct((16, 128), F32),),
        in_specs=[hbm, hbm, hbm, hbm, hbm, pl.BlockSpec(memory_space=pltpu.SMEM), vmem],
        out_specs=(hbm, hbm, hbm, vmem),
        scratch_shapes=scratch,
        compiler_params=pltpu.CompilerParams(
            collective_id=0, has_side_effects=True, vmem_limit_bytes=62 * MIB
        ),
        cost_estimate=pl.CostEstimate(flops=20 * 10**9, bytes_accessed=16 * MIB, transcendentals=0),
        name="selected_inverse",
    )(
        root_inverse, middle_inverse, middle_panel, lower_root, lower_middle, block_pattern,
        lower_diagonal.reshape(8, 128),
    )
    return pl.pallas_call(
        finish,
        out_shape=(
            blocks[0], jax.ShapeDtypeStruct((512,), F32), blocks[1], blocks[2], jax.ShapeDtypeStruct((1024,), F32),
        ),
        in_specs=[hbm, hbm, hbm, hbm],
        out_specs=(hbm, vmem, hbm, hbm, vmem),
        scratch_shapes=[pltpu.VMEM(x.shape, F32) for x in (first, root, par, total)] + [dma((2, 4))],
        compiler_params=pltpu.CompilerParams(vmem_limit_bytes=62 * MIB),
        name="hand_over",
    )(first, root, par, total)


def solution(mesh):
    in_specs = (
        P("grid", "leaf"),
        P("grid", "leaf"),
        P("grid", "leaf"),
        P("grid", "leaf"),
        P(None, "leaf"),
        P(),
        P("leaf"),
    )
    out_specs = (P("grid", "leaf"), P("leaf"), P("grid", "leaf"), P("grid", "leaf"), P("leaf"))
    return jax.shard_map(local, mesh=mesh, in_specs=in_specs, out_specs=out_specs, check_vma=False)
```

profile of v0, /device:TPU:1, one launch (start us, length us, event | category | flops | bytes accessed | tf_op | source)
XLA Modules:
  0.0 135.9 jit_solution(14302402037732437593)
XLA Ops:
  0.6 131.9 %selected_inverse.1 = (f32[256,512]{1,0:T(8,128)}, f32[256,1024]{1,0:T(8,128)}, f32[128,1024]{1,0:T(8,128)}, f32[16,128]{1,0:T(8,128)}) custom-call(f32[256,512]{1,0:T(8,128)} %s_hbm.1, f32[128,512]{1,0:T(8,128)} %minv_hbm.1, f32[256,512]{1,0:T(8,128)} %p_hbm.1, f32[256,1024]{1,0:T(8,128)} %l_hbm.1, f32[2048,1024]{1,0:T(8,128)} %m_hbm.1, s32[4,32]{1,0:T(4,128)} %pattern.1, ...), custom_call_target="tpu_custom_call" | custom-call | flops 20000000000 | bytes 16777216 | tf_op jit(solution)/shard_map/selected_inverse/pallas_call | solution.py:603
  132.5 3.2 %hand_over.1 = (f32[256,512]{1,0:T(8,128)}, f32[512]{0:T(512)}, f32[256,1024]{1,0:T(8,128)}, f32[128,1024]{1,0:T(8,128)}, f32[1024]{0:T(1024)}) custom-call(f32[256,512]{1,0:T(8,128)} %get-tuple-element.9.first, f32[256,1024]{1,0:T(8,128)} %get-tuple-element.10.root, f32[128,1024]{1,0:T(8,128)} %get-tuple-element.11.par, f32[16,128]{1,0:T(8,128)} %get-tuple-element.12.total_hbm), custom_call_target="tpu_custom_call" | custom-call | tf_op jit(solution)/shard_map/hand_over/pallas_call | solution.py:618
where the time goes:
time: 136 us
  Pallas kernels  135 us (99%)
    pallas_call x1, Pallas kernels, local(): pl.pallas_call(kernel, out_shape=blocks + (jax.ShapeDtypeStruct((16, 128)...  132 us
    pallas_call x1, Pallas kernels, local(): pl.pallas_call(finish, out_shape=(blocks[0], jax.ShapeDtypeStruct((512,),...  3.2 us

commit v1 on v0

--- a/solution.py
+++ b/solution.py
@@ -88,6 +88,21 @@
     for k in range(1, 4):
         x = (a * 2 + b + k) % 4
         greet(device(z, x // 2, y, x % 2, c))
+
+    own_l = pltpu.make_async_copy(l_hbm, l_buf.at[0, here_rows], loc.at[4])
+    own_l.start()
+
+    def m_load(i):
+        return pltpu.make_async_copy(m_hbm.at[pl.ds(i * 256, 256)], m_stage.at[i % 2], mst.at[i % 2])
+
+    m_load(0).start()
+    m_load(1).start()
+
+    own_l.wait()
+    for i in range(2):
+        keep = pattern[leaf // 2, grid * 2 + i].astype(F32)
+        l_buf[0, half_rows(i)] = l_buf[0, half_rows(i)] * keep
+
     pl.semaphore_wait(bar, 20)
 
     def own_s(h):
@@ -128,8 +143,6 @@
 
     step_start(0)
 
-    own_l = pltpu.make_async_copy(l_hbm, l_buf.at[0, here_rows], loc.at[4])
-    own_l.start()
 
     def y_own(src, buf, ss, rs, h, k):
         return remote(src, buf.at[k, half_rows(h)], ss.at[h, k], rs.at[h, k], at_y(k))
@@ -153,12 +166,6 @@
     own_t.start()
     own_m.start()
 
-    def m_load(i):
-        return pltpu.make_async_copy(m_hbm.at[pl.ds(i * 256, 256)], m_stage.at[i % 2], mst.at[i % 2])
-
-    m_load(0).start()
-    m_load(1).start()
-
     def p_side(k):
         return remote(p_hbm if k == 0 else p_col.at[k, here_rows], p_col.at[k, here_rows],
                       ps_s.at[k], ps_r.at[k], sibling)
@@ -167,11 +174,6 @@
         return remote(l_buf.at[k, here_rows], l_buf.at[k, here_rows], ls_s.at[k], ls_r.at[k], sibling)
 
     p_side(0).start()
-
-    own_l.wait()
-    for i in range(2):
-        keep = pattern[leaf // 2, grid * 2 + i].astype(F32)
-        l_buf[0, half_rows(i)] = l_buf[0, half_rows(i)] * keep
 
     def split_m(i):
         m_load(i).wait()
@@ -328,6 +330,9 @@
     y_on(p_col, py_s, py_r, 0).start()
     p_own(1, 3).wait_recv()
     y_on(p_col, py_s, py_r, 1).start()
+    for h, k in ((0, 1), (1, 3), (1, 1), (0, 3)):
+        l_own(h, k).start()
+    l_side(0).start()
     s_here(0)
     split_m(3)
     step_relay(1)
@@ -335,9 +340,6 @@
     p_side(1).start()
     p_own(0, 3).wait_recv()
     p_side(3).start()
-    for h, k in ((0, 1), (1, 3), (1, 1), (0, 3)):
-        l_own(h, k).start()
-    l_side(0).start()
     split_m(4)
     s_on(0)
     s_here(1)
@@ -350,6 +352,7 @@
     y_on(p_col, py_s, py_r, 1).wait_recv()
     p_side(2).start()
     split_m(6)
+    l_ready(0)
     p_side(2).wait_recv()
     split_rows(p_col, p_hi, p_lo, 2)
     f_chunk(0, 0, True)
@@ -358,7 +361,7 @@
     split_m(7)
     f_last(0)
     f_chunk(1, 0, True)
-    l_ready(0)
+
     l_own(0, 1).wait_recv()
     y_on(l_buf, ly_s, ly_r, 0).start()
     l_own(1, 3).wait_recv()
@@ -418,17 +421,26 @@
             else:
                 came.wait_recv()
             hi, lo = high_low(ft[far, cc, h].T)
-            ft_split[h, k, 0:256, cc * 128:cc * 128 + 128] = hi
-            ft_split[h, k, 256:512, cc * 128:cc * 128 + 128] = lo
+            ft_split[k, 0:256, h * 256 + cc * 128:h * 256 + cc * 128 + 128] = hi
+            ft_split[k, 256:512, h * 256 + cc * 128:h * 256 + cc * 128 + 128] = lo
         rows = slice(h * 256, h * 256 + 256)
-        accumulate(t_part, ft_split.at[h, k], p_hi.at[k, rows], p_lo.at[k, rows], first)
-
-    def q_chunk(h, k, first):
-        rows = slice(h * 256, h * 256 + 256)
-        accumulate(q_part, ft_split.at[h, k], l_hi.at[k, rows], l_lo.at[k, rows], first)
+        accumulate(t_part, ft_split.at[k, :, rows], p_hi.at[k, rows], p_lo.at[k, rows], first)
 
     for k in (0, 1, 3, 2):
         t_chunk(0, k, k == 0)
+
+    for k in (0, 1, 3, 2):
+        t_chunk(1, k, False)
+    tx.start()
+    for k in range(4):
+        accumulate(q_part, ft_split.at[k], l_hi.at[k], l_lo.at[k], k == 0)
+    own_t.wait()
+    tx.wait_recv()
+    t_row[0] = t_row[0] + (t_part[own_rows] + t_recv[...])
+    tr(1).start()
+    tr(2).start()
+    qx = remote(q_part.at[other_rows], q_recv, qx_s.at[0], qx_r.at[0], partner)
+    qx.start()
 
     for k in range(4):
         for h in range(2):
@@ -440,21 +452,6 @@
                     a_tmp[h * 128:h * 128 + 128, at:at + 128] = hi[:, part]
                     a_tmp[256 + h * 128:256 + h * 128 + 128, at:at + 128] = lo[:, part]
         accumulate(fm, a_tmp, m_hi.at[flip(idx, k)], m_lo.at[flip(idx, k)], k == 0)
-    for k in (0, 1, 3, 2):
-        q_chunk(0, k, k == 0)
-    for k in (0, 1, 3, 2):
-        t_chunk(1, k, False)
-    tx.start()
-    for k in (0, 1, 3, 2):
-        q_chunk(1, k, False)
-    own_t.wait()
-    tx.wait_recv()
-    t_row[0] = t_row[0] + (t_part[own_rows] + t_recv[...])
-    tr(1).start()
-    tr(2).start()
-    qx = remote(q_part.at[other_rows], q_recv, qx_s.at[0], qx_r.at[0], partner)
-    qx.start()
-
     row_at = grid * 128 + lax.broadcasted_iota(jnp.int32, (128, 512), 0)
     col_at = idx * 512 + lax.broadcasted_iota(jnp.int32, (128, 512), 1)
     mid = jnp.sum(jnp.where(row_at == col_at, t_row[0], 0.0), axis=0, keepdims=True)
@@ -462,15 +459,8 @@
         sums[0, 8 + i:9 + i] = mid[:, i * 128:i * 128 + 128]
         sums[0, 12 + i:13 + i] = jnp.zeros((1, 128), F32)
 
-    for k in range(4):
-        if k:
-            tr(k).wait_recv()
-        if k == 1:
-            tr(3).start()
-        hi, lo = high_low(t_row[k])
-        t_tmp[0:128] = hi
-        t_tmp[128:256] = lo
-        accumulate(tm, t_tmp, m_hi.at[flip(idx, k)], m_lo.at[flip(idx, k)], k == 0)
+    tr(1).wait_recv()
+    tr(3).start()
 
     def root_done(h):
         return pltpu.make_async_copy(r_recv.at[h], root_hbm.at[pl.ds(h * 128, 128)], loc.at[9 + h])
@@ -483,6 +473,15 @@
         r_recv[h] = -root
         root_done(h).start()
         low += jnp.sum(l_buf[0, half_rows(h)] * root, axis=0, keepdims=True)
+
+    for k in range(4):
+        if k > 1:
+            tr(k).wait_recv()
+        hi, lo = high_low(t_row[k])
+        t_tmp[0:128] = hi
+        t_tmp[128:256] = lo
+        accumulate(tm, t_tmp, m_hi.at[flip(idx, k)], m_lo.at[flip(idx, k)], k == 0)
+
     own_m.wait()
     qx.wait_recv()
     par = tm[...] - (q_part[own_rows] + q_recv[...])
@@ -589,7 +588,7 @@
         pltpu.VMEM(shape, BF16)
         for shape in (
             (4, 2, 512, 512), (4, 512, 1024), (4, 512, 1024), (4, 512, 1024), (4, 512, 1024),
-            (4, 512, 512), (4, 512, 512), (512, 512), (256, 512), (2, 4, 512, 256),
+            (4, 512, 512), (4, 512, 512), (512, 512), (256, 512), (4, 512, 512),
         )
     ] + [
         dma(shape)

time: 136 us -> 136 us (level)
  no operation moved by 1% of the time
where the time goes in v1:
time: 136 us
  Pallas kernels  135 us (99%)
    pallas_call x1, Pallas kernels, local(): pl.pallas_call(kernel, out_shape=blocks + (jax.ShapeDtypeStruct((16, 128)...  132 us
    pallas_call x1, Pallas kernels, local(): pl.pallas_call(finish, out_shape=(blocks[0], jax.ShapeDtypeStruct((512,),...  3.2 us

profile of v1, /device:TPU:1, one launch (start us, length us, event | category | flops | bytes accessed | tf_op | source)
XLA Modules:
  0.0 135.9 jit_solution(8617278824984182404)
XLA Ops:
  0.6 131.9 %selected_inverse.1 = (f32[256,512]{1,0:T(8,128)}, f32[256,1024]{1,0:T(8,128)}, f32[128,1024]{1,0:T(8,128)}, f32[16,128]{1,0:T(8,128)}) custom-call(f32[256,512]{1,0:T(8,128)} %s_hbm.1, f32[128,512]{1,0:T(8,128)} %minv_hbm.1, f32[256,512]{1,0:T(8,128)} %p_hbm.1, f32[256,1024]{1,0:T(8,128)} %l_hbm.1, f32[2048,1024]{1,0:T(8,128)} %m_hbm.1, s32[4,32]{1,0:T(4,128)} %pattern.1, ...), custom_call_target="tpu_custom_call" | custom-call | flops 20000000000 | bytes 16777216 | tf_op jit(solution)/shard_map/selected_inverse/pallas_call | solution.py:602
  132.5 3.2 %hand_over.1 = (f32[256,512]{1,0:T(8,128)}, f32[512]{0:T(512)}, f32[256,1024]{1,0:T(8,128)}, f32[128,1024]{1,0:T(8,128)}, f32[1024]{0:T(1024)}) custom-call(f32[256,512]{1,0:T(8,128)} %get-tuple-element.9.first, f32[256,1024]{1,0:T(8,128)} %get-tuple-element.10.root, f32[128,1024]{1,0:T(8,128)} %get-tuple-element.11.par, f32[16,128]{1,0:T(8,128)} %get-tuple-element.12.total_hbm), custom_call_target="tpu_custom_call" | custom-call | tf_op jit(solution)/shard_map/hand_over/pallas_call | solution.py:617
